TPU v7x, 32 devices: a whole 2x2x4 slice. The times are simulated.
32 devices in a mesh: group: 2 (over y), expert: 16 (over z, x, core), tensor: 1.
Axes of the slice: x: 2, y: 2, z: 4, core: 2. Of those that a mesh axis runs over, the one named last changes fastest.
Arguments:
- residual: bfloat16 [2048, 3584], P(('group', 'expert'), 'tensor'), parts along dimension 0, may hold values from -6 to 6
- attn_partial: bfloat16 [1, 2048, 3584], P('tensor', ('group', 'expert')), parts along dimension 1, may hold values from -6 to 6
- norm_gain: float32 [3584], replicated, may hold values from 0.25 to 1.75
- router_weight: bfloat16 [3584, 16], P('tensor'), may hold values from -0.1875 to 0.1875
- expert_ids: int32 [2048, 8], P(('group', 'expert')), parts along dimension 0, may hold values from 0 to 15, all different within a row; in each aligned block of 64 rows (0 to 63, 64 to 127, ...) at most 56 rows name the same one
- expert_weight: bfloat16 [16, 3584, 1024], P('expert', None, 'tensor'), may hold values from -0.1875 to 0.1875
Outputs:
- layer_out: bfloat16 [2048, 3584], P(('group', 'expert'), 'tensor'), parts along dimension 0
There are 2 independent parts, one for each index of `group`. A program takes and returns all parts, laid end to end along the dimension named above; an argument that names none is the same for every part. Nothing has to cross between parts.
Inputs may be any that keep to these rules, and one draw needn't show every extreme that they name: `expert_ids`: the 8 experts of a row are distinct. Among the rows of one device (aligned blocks of 64 rows) no expert is named more than 56 times, a bound that some block reaches.
All inputs are finite; a program needn't handle non-finite values.
Results may differ from a plain program's by a relative error of at most 0.015.
Values may be sent and summed in bfloat16 or wider, within the bound.
A program may use at most 64 MiB of HBM per device.

v0:
```python
import jax
import jax.numpy as jnp
from jax import lax
from jax.sharding import PartitionSpec as P

QBLOCK = 128


EPS = 1e-06
ROUTE_SCALE = 2.5


def encode(values):
    row_count, columns = values.shape
    blocks = values.astype(jnp.float32).reshape(row_count, columns // QBLOCK, QBLOCK)
    largest = jnp.max(jnp.abs(blocks), axis=-1)
    block_scale = ((largest + EPS) / 448.0).astype(jnp.bfloat16)
    encoded = (blocks / block_scale.astype(jnp.float32)[:, :, None]).astype(jnp.bfloat16)
    return (encoded.reshape(row_count, columns), block_scale)


def decode(encoded, block_scale):
    leading = encoded.shape[:-1]
    columns = encoded.shape[-1]
    blocks = encoded.astype(jnp.float32).reshape(leading + (columns // QBLOCK, QBLOCK))
    restored = (blocks * block_scale.astype(jnp.float32)[..., None]).astype(jnp.bfloat16)
    return restored.reshape(leading + (columns,))


def local(residual, attn_partial, norm_gain, router_weight, expert_ids, expert_weight):
    row_count, share_width = residual.shape
    tensor_count = lax.axis_size("tensor")
    model_width = share_width * tensor_count
    expert_count = router_weight.shape[1]
    top_count = expert_ids.shape[1]
    capacity = min(row_count, max(2, 7 * row_count * top_count // (4 * expert_count)))
    first_column = lax.axis_index("tensor") * share_width
    partial_attn = attn_partial[0].astype(jnp.float32)
    full_residual = lax.all_gather(residual, "tensor", axis=1, tiled=True)
    attention = lax.psum(partial_attn.astype(jnp.bfloat16), "tensor").astype(jnp.float32)
    stream = full_residual.astype(jnp.float32) + attention
    meansq = jnp.mean(stream * stream, axis=1, keepdims=True)
    normed = (stream * lax.rsqrt(meansq + EPS) * norm_gain).astype(jnp.bfloat16)
    normed_share = lax.dynamic_slice_in_dim(normed, first_column, share_width, 1)
    stream_share = lax.dynamic_slice_in_dim(stream, first_column, share_width, 1)
    logits = lax.psum(
        jnp.dot(normed_share, router_weight, preferred_element_type=jnp.float32).astype(
            jnp.bfloat16
        ),
        "tensor",
    ).astype(jnp.float32)
    affinity = jax.nn.sigmoid(logits)
    chosen = expert_ids[:, :, None] == jnp.arange(expert_count, dtype=jnp.int32)[None, None, :]
    picked = jnp.sum(jnp.where(chosen, affinity[:, None, :], 0.0), axis=2)
    gate_values = ROUTE_SCALE * picked / jnp.sum(picked, axis=1, keepdims=True)
    encoded, block_scale = encode(normed)
    flat_ids = expert_ids.reshape(-1)
    onehot = (flat_ids[:, None] == jnp.arange(expert_count, dtype=jnp.int32)[None, :]).astype(
        jnp.int32
    )
    before = jnp.cumsum(onehot, axis=0) - onehot
    slot_index = jnp.sum(before * onehot, axis=1)
    target_slot = flat_ids * capacity + slot_index
    source_row = jnp.arange(row_count * top_count, dtype=jnp.int32) // top_count
    send_codes = (
        jnp.zeros((expert_count * capacity, encoded.shape[1]), jnp.bfloat16)
        .at[target_slot]
        .set(encoded[source_row])
    )
    send_scales = (
        jnp.zeros((expert_count * capacity, block_scale.shape[1]), jnp.bfloat16)
        .at[target_slot]
        .set(block_scale[source_row])
    )
    send_codes = send_codes.reshape(expert_count, 1, capacity, encoded.shape[1])
    send_scales = send_scales.reshape(expert_count, 1, capacity, block_scale.shape[1])
    codes_in = lax.all_to_all(send_codes, "expert", split_axis=0, concat_axis=1, tiled=True)
    scales_in = lax.all_to_all(send_scales, "expert", split_axis=0, concat_axis=1, tiled=True)
    inputs = decode(codes_in, scales_in)
    leading = inputs.shape[:-1]
    flat_rows = inputs.reshape(-1, model_width)
    w_expert = expert_weight[0]
    hidden = jax.nn.silu(jnp.dot(flat_rows, w_expert, preferred_element_type=jnp.float32)).astype(
        jnp.bfloat16
    )
    output = lax.dot_general(
        hidden, w_expert, (((1,), (1,)), ((), ())), preferred_element_type=jnp.float32
    ).astype(jnp.bfloat16)
    halves = output.reshape(leading + (tensor_count, 1, share_width))
    returned = lax.all_to_all(
        lax.all_to_all(halves, "expert", split_axis=1, concat_axis=0, tiled=True),
        "tensor",
        split_axis=3,
        concat_axis=4,
        tiled=True,
    )
    expert_out = jnp.sum(returned.astype(jnp.float32), axis=(3, 4)).astype(jnp.bfloat16)
    taken = expert_out.reshape(expert_count * capacity, share_width)[target_slot]
    taken = taken.reshape(row_count, top_count, share_width)
    moe_share = jnp.einsum("rk,rkd->rd", gate_values, taken.astype(jnp.float32))
    return (stream_share + moe_share).astype(jnp.bfloat16)


def solution(mesh):
    placed = (
        P(("group", "expert"), "tensor"),
        P("tensor", ("group", "expert"), None),
        P(),
        P("tensor", None),
        P(("group", "expert"), None),
        P("expert", None, "tensor"),
    )
    return jax.shard_map(
        local,
        mesh=mesh,
        in_specs=placed,
        out_specs=P(("group", "expert"), "tensor"),
        check_vma=False,
    )
```

profile of v0, /device:TPU:15, one launch (start us, length us, event | category | flops | bytes accessed | tf_op | source)
XLA Modules:
  0.0 385.4 jit_solution(5509032993525898569)
XLA Ops:
  0.0 0.7 broadcast_multiply_fusion
  0.7 0.8 copy.43
  1.7 1.4 multiply_reduce_fusion
  3.2 0.1 mul.76
  3.3 1.2 reduce-window.6
  4.5 0.2 slice_reduce_fusion
  4.7 1.4 convert_abs_fusion
  6.1 0.2 abs.7
  6.3 0.3 reduce_max.9
  6.7 0.1 fusion.30
  6.8 3.1 scatter_custom_fusion.1
  9.9 0.2 copy.47
  10.1 0.8 reshape.246
  10.9 7.1 %all-to-all-start.1 = ((bf16[16,2,784]{2,1,0:T(2,128)(2,1)}), bf16[16,2,784]{2,1,0:T(2,128)(2,1)S(1)}, u32[]{:S(2)}, u32[]{:S(2)}) async-start(bf16[16,2,784]{2,1,0:T(2,128)(2,1)} %reshape.246), calls=%async_computation.1 | async-start | bytes 114688 | tf_op jit(solution)/shard_map/all_to_all | solution.py:78
  18.0 0.3 div.55
  18.3 0.6 fusion.23
  18.9 20.2 %scatter_custom_fusion = bf16[896,3584]{1,0:T(8,128)(2,1)} fusion(s32[512]{0:T(512)S(1)} %bitcast.81, bf16[64,3584]{1,0:T(8,128)(2,1)S(1)} %fusion.23, s32[1024]{0:T(1024)S(1)} %pad_clamp_fusion.1, bf16[]{:T(256)} %constant.44.clone.1), kind=kCustom, calls=%fused_computation.15 | custom fusion | bytes 6422530 | tf_op jit(solution)/shard_map/scatter | solution.py:68
  39.2 6.4 %all-to-all-start = ((bf16[16,1,56,3584]{3,2,1,0:T(8,128)(2,1)}), bf16[16,1,56,3584]{3,2,1,0:T(8,128)(2,1)}, u32[]{:S(2)}, u32[]{:S(2)}) async-start(bf16[16,1,56,3584]{3,2,1,0:T(8,128)(2,1)} %bitcast.74), calls=%async_computation | async-start | bytes 12845056 | tf_op jit(solution)/shard_map/all_to_all | solution.py:77
  45.5 0.2 reshape.247
  45.8 0.2 copy.48
  46.0 139.6 %all-to-all-done = bf16[16,1,56,3584]{3,2,1,0:T(8,128)(2,1)} async-done(((bf16[16,1,56,3584]{3,2,1,0:T(8,128)(2,1)}), bf16[16,1,56,3584]{3,2,1,0:T(8,128)(2,1)}, u32[]{:S(2)}, u32[]{:S(2)}) %all-to-all-start) | async-done | bytes 6422560 | tf_op jit(solution)/shard_map/all_to_all | solution.py:77
  185.6 12.2 %reshape.189 = f32[16,56,28,128]{3,2,1,0:T(8,128)} reshape(bf16[16,1,56,3584]{3,2,1,0:T(8,128)(2,1)} %all-to-all-done) | data formatting | bytes 19267584 | tf_op jit(solution)/shard_map/convert_element_type | solution.py:25
  197.8 7.4 %multiply_convert_fusion = bf16[16,56,28,128]{3,2,1,0:T(8,128)(2,1)S(1)} fusion(f32[16,56,28,128]{3,2,1,0:T(8,128)} %reshape.189, f32[16,56,28]{2,1,0:T(8,128)S(1)} %copy.48), kind=kLoop, calls=%fused_computation.5 | loop fusion | flops 6422528 | bytes 19367936 | tf_op jit(solution)/shard_map/convert_element_type | solution.py:26
  205.2 9.8 %multiply_convert_fusion.1 = bf16[896,1024]{1,0:T(8,128)(2,1)S(1)} fusion(bf16[1,3584,1024]{2,1,0:T(8,128)(2,1)} %param.11, bf16[112,8,28,128]{3,2,1,0:T(8,128)(2,1)S(1)} %bitcast.75), kind=kOutput, calls=%fused_computation.17 | convolution fusion | flops 6581256192 | bytes 15597568 | tf_op jit(solution)/shard_map/dot_general | solution.py:83
  215.1 8.9 %fusion.4 = bf16[896,3584]{1,0:T(8,128)(2,1)} fusion(bf16[896,1024]{1,0:T(8,128)(2,1)S(1)} %multiply_convert_fusion.1, bf16[1,3584,1024]{2,1,0:T(8,128)(2,1)S(1)} %bitcast.86), kind=kOutput, calls=%fused_computation.10 | convolution fusion | flops 6579879936 | bytes 15597568 | tf_op jit(solution)/shard_map/dot_general | solution.py:86
  223.9 5.4 %all-to-all-start.2 = ((bf16[1,16,56,1,1,3584]{5,2,4,3,0,1:T(8,128)(2,1)}), bf16[1,16,56,1,1,3584]{5,2,4,3,0,1:T(8,128)(2,1)}, u32[]{:S(2)}, u32[]{:S(2)}) async-start(bf16[1,16,56,1,1,3584]{5,2,4,3,0,1:T(8,128)(2,1)} %bitcast.76), calls=%async_computation.2 | async-start | bytes 12845056 | tf_op jit(solution)/shard_map/all_to_all | solution.py:91
  229.4 0.2 fusion.22
  229.7 0.1 copy.50
  229.8 139.6 %all-to-all-done.2 = bf16[1,16,56,1,1,3584]{5,2,4,3,0,1:T(8,128)(2,1)} async-done(((bf16[1,16,56,1,1,3584]{5,2,4,3,0,1:T(8,128)(2,1)}), bf16[1,16,56,1,1,3584]{5,2,4,3,0,1:T(8,128)(2,1)}, u32[]{:S(2)}, u32[]{:S(2)}) %all-to-all-start.2) | async-done | bytes 6422560 | tf_op jit(solution)/shard_map/all_to_all | solution.py:91
  369.4 11.7 %gather_fusion = bf16[512,3584]{1,0:T(8,128)(2,1)} fusion(bf16[896,3584]{1,0:T(8,128)(2,1)} %bitcast.12, s32[1024]{0:T(1024)S(1)} %pad_clamp_fusion), kind=kCustom, calls=%fused_computation.2 | custom fusion | bytes 7342080 | tf_op jit(solution)/shard_map/gather | solution.py:98
  381.1 3.1 fusion.9
  384.3 0.9 fusion.24
  (29 shorter events, 0.5 us)
Async XLA Ops:
  0.0 229.3 %copy-start = (bf16[3584,16]{0,1:T(8,128)(2,1)S(1)}, bf16[3584,16]{0,1:T(8,128)(2,1)}, u32[]{:S(2)}) copy-start(bf16[3584,16]{0,1:T(8,128)(2,1)} %param.9) | copy-start | bytes 344068
  10.9 28.3 %all-to-all-start.1 = ((bf16[16,2,784]{2,1,0:T(2,128)(2,1)}), bf16[16,2,784]{2,1,0:T(2,128)(2,1)S(1)}, u32[]{:S(2)}, u32[]{:S(2)}) async-start(bf16[16,2,784]{2,1,0:T(2,128)(2,1)} %reshape.246), calls=%async_computation.1 | async-start | bytes 114688 | tf_op jit(solution)/shard_map/all_to_all | solution.py:78
  39.2 146.5 %all-to-all-start = ((bf16[16,1,56,3584]{3,2,1,0:T(8,128)(2,1)}), bf16[16,1,56,3584]{3,2,1,0:T(8,128)(2,1)}, u32[]{:S(2)}, u32[]{:S(2)}) async-start(bf16[16,1,56,3584]{3,2,1,0:T(8,128)(2,1)} %bitcast.74), calls=%async_computation | async-start | bytes 12845056 | tf_op jit(solution)/shard_map/all_to_all | solution.py:77
  197.8 17.2 %slice-start = ((s8[7340032]{0:T(1024)(128)(4,1)}), s8[4194304]{0:T(1024)(128)(4,1)S(1)}, s32[]{:S(2)}) async-start(s8[7340032]{0:T(1024)(128)(4,1)} %bitcast.85), calls=%async_computation.3 | async-start | bytes 8388608
  205.2 9.8 %slice-start.1 = ((s8[7340032]{0:T(1024)(128)(4,1)}), s8[3145728]{0:T(1024)(128)(4,1)S(1)}, s32[]{:S(2)}) async-start(s8[7340032]{0:T(1024)(128)(4,1)} %bitcast.85), calls=%async_computation.4 | async-start | bytes 6291456
  223.9 5.7 %copy-start.3 = (s32[64,8]{0,1:T(8,128)S(1)}, s32[64,8]{0,1:T(8,128)}, u32[]{:S(2)}) copy-start(s32[64,8]{0,1:T(8,128)} %param.10) | copy-start | bytes 6148
  223.9 145.5 %all-to-all-start.2 = ((bf16[1,16,56,1,1,3584]{5,2,4,3,0,1:T(8,128)(2,1)}), bf16[1,16,56,1,1,3584]{5,2,4,3,0,1:T(8,128)(2,1)}, u32[]{:S(2)}, u32[]{:S(2)}) async-start(bf16[1,16,56,1,1,3584]{5,2,4,3,0,1:T(8,128)(2,1)} %bitcast.76), calls=%async_computation.2 | async-start | bytes 12845056 | tf_op jit(solution)/shard_map/all_to_all | solution.py:91
  369.4 14.8 %copy-start.1 = (bf16[64,3584]{1,0:T(8,128)(2,1)S(1)}, bf16[64,3584]{1,0:T(8,128)(2,1)}, u32[]{:S(2)}) copy-start(bf16[64,3584]{1,0:T(8,128)(2,1)} %param.6) | copy-start | bytes 1376260
  369.4 14.8 %copy-start.2 = (bf16[1,64,3584]{2,1,0:T(8,128)(2,1)S(1)}, bf16[1,64,3584]{2,1,0:T(8,128)(2,1)}, u32[]{:S(2)}) copy-start(bf16[1,64,3584]{2,1,0:T(8,128)(2,1)} %param.7) | copy-start | bytes 1376260
where the time goes:
time: 390 us; the launch traced here: 385 us
  waiting for transfers between devices  279 us (72%)
  local copies, waits for them, and re-layouts  50.6 us (13%)
  matrix products  22 us (6%)
  starting transfers between devices  18.8 us (5%)
  other arithmetic  14.2 us (4%)
    all_to_all x1, waiting for transfers between devices, local(): lax.all_to_all(halves, 'expert', split_axis=1, concat_axis=0, tiled=True)  140 us
    all_to_all x1, waiting for transfers between devices, local(): lax.all_to_all(send_codes, 'expert', split_axis=0, concat_axis=1, tiled=T...  140 us
    scatter x1, local copies, waits for them, and re-layouts, local(): send_codes = jnp.zeros((expert_count * capacity, encoded.shape[1]), jnp.b...  20.2 us
    convert_element_type x1, local copies, waits for them, and re-layouts, decode(): encoded.astype(jnp.float32).reshape(leading + (columns // QBLOCK, QBLOCK))  12.2 us
    gather x1, local copies, waits for them, and re-layouts, local(): expert_out.reshape(expert_count * capacity, share_width)[target_slot]  11.7 us
    dot_general x1, matrix products, local(): jnp.dot(flat_rows, w_expert, preferred_element_type=jnp.float32)  9.79 us
    dot_general x1, matrix products, local(): lax.dot_general(hidden, w_expert, (((1,), (1,)), ((), ())), preferred_ele...  8.86 us
  transfers between devices with their start and end apart: 3, of which 2 were waited for; matrix products, arithmetic and copies ran while one was open for 6% of the time, Pallas kernels for 0%

commit v1 on v0

--- a/solution.py
+++ b/solution.py
@@ -101,6 +101,48 @@
     return (stream_share + moe_share).astype(jnp.bfloat16)
 
 
+def local_rows(residual, attn_partial, norm_gain, router_weight, expert_ids):
+    expert_count = router_weight.shape[1]
+    stream = residual.astype(jnp.float32) + attn_partial[0].astype(jnp.float32)
+    meansq = jnp.mean(stream * stream, axis=1, keepdims=True)
+    normed = (stream * lax.rsqrt(meansq + EPS) * norm_gain).astype(jnp.bfloat16)
+    logits = jnp.dot(normed, router_weight, preferred_element_type=jnp.float32)
+    affinity = jax.nn.sigmoid(logits)
+    chosen = expert_ids[:, :, None] == jnp.arange(expert_count, dtype=jnp.int32)[None, None, :]
+    picked = jnp.where(jnp.any(chosen, axis=1), affinity, 0.0)
+    gates = ROUTE_SCALE * picked / jnp.sum(picked, axis=1, keepdims=True)
+    encoded, block_scale = encode(normed)
+    restored = decode(encoded, block_scale)
+    return stream, gates, restored
+
+
+def local_dense(residual, attn_partial, norm_gain, router_weight, expert_ids, expert_weight):
+    stream, gates, restored = local_rows(
+        residual, attn_partial, norm_gain, router_weight, expert_ids
+    )
+    rows = lax.all_gather(restored, "expert", axis=0, tiled=True)
+    all_gates = lax.all_gather(gates, "expert", axis=0, tiled=True)
+    gate = lax.dynamic_slice_in_dim(all_gates, lax.axis_index("expert"), 1, 1)
+    w_expert = expert_weight[0]
+    hidden = jax.nn.silu(jnp.dot(rows, w_expert, preferred_element_type=jnp.float32)).astype(
+        jnp.bfloat16
+    )
+    output = lax.dot_general(
+        hidden, w_expert, (((1,), (1,)), ((), ())), preferred_element_type=jnp.float32
+    ).astype(jnp.bfloat16)
+    share = (output.astype(jnp.float32) * gate).astype(jnp.bfloat16)
+    moe = lax.psum_scatter(share, "expert", scatter_dimension=0, tiled=True)
+    return (stream + moe.astype(jnp.float32)).astype(jnp.bfloat16)
+
+
+def dense_fits(mesh, row_count, expert_count, top_count):
+    return (
+        mesh.shape["tensor"] == 1
+        and mesh.shape["expert"] == expert_count
+        and expert_count <= 4 * top_count
+    )
+
+
 def solution(mesh):
     placed = (
         P(("group", "expert"), "tensor"),
@@ -110,10 +152,15 @@
         P(("group", "expert"), None),
         P("expert", None, "tensor"),
     )
-    return jax.shard_map(
-        local,
-        mesh=mesh,
-        in_specs=placed,
-        out_specs=P(("group", "expert"), "tensor"),
-        check_vma=False,
-    )
+
+    def run(residual, attn_partial, norm_gain, router_weight, expert_ids, expert_weight):
+        dense = dense_fits(mesh, residual.shape[0], router_weight.shape[1], expert_ids.shape[1])
+        return jax.shard_map(
+            local_dense if dense else local,
+            mesh=mesh,
+            in_specs=placed,
+            out_specs=P(("group", "expert"), "tensor"),
+            check_vma=False,
+        )(residual, attn_partial, norm_gain, router_weight, expert_ids, expert_weight)
+
+    return run

time: 390 us -> 208 us (0.53)
  the two profiles are of different devices: /device:TPU:15 before, /device:TPU:0 now
where the time goes in v1:
time: 208 us
  waiting for transfers between devices  137 us (66%)
  matrix products  25.8 us (12%)
  blocking collectives  23.9 us (11%)
  between operations  13.5 us (6%)
  other arithmetic  6.51 us (3%)
    reduce_scatter x1, waiting for transfers between devices, local_dense(): moe = lax.psum_scatter(share, 'expert', scatter_dimension=0, tiled=True)  90.3 us
    all_gather x1, waiting for transfers between devices, local_dense(): rows = lax.all_gather(restored, 'expert', axis=0, tiled=True)  46.9 us
    all_gather x1, blocking collectives, local_dense(): all_gates = lax.all_gather(gates, 'expert', axis=0, tiled=True)  23.9 us
    dot_general x1, matrix products, local_dense(): lax.dot_general(hidden, w_expert, (((1,), (1,)), ((), ())), preferred_ele...  12.9 us
    dot_general x1, matrix products, local_dense(): jnp.dot(rows, w_expert, preferred_element_type=jnp.float32)  12.7 us
  transfers between devices with their start and end apart: 2, of which 2 were waited for; matrix products, arithmetic and copies ran while one was open for 0% of the time, Pallas kernels for 0%

profile of v1, /device:TPU:0, one launch (start us, length us, event | category | flops | bytes accessed | tf_op | source)
XLA Modules:
  0.0 207.8 jit_solution(3176271018803685739)
XLA Ops:
  6.5 0.0 copy-start
  6.5 0.0 copy-start.3
  6.5 0.0 all-gather.3.cloned.1.call-start
  6.5 1.4 multiply_reduce_fusion
  8.0 1.4 convert_abs_fusion
  9.4 0.2 abs.7
  9.6 0.3 reduce_max.9
  10.0 0.3 div.42
  10.3 1.3 fusion.12
  11.6 0.0 all-gather.3.cloned.1.call-update
  11.7 0.0 reduce-scatter.2.cloned.1.call-start
  11.7 0.0 copy-done.3
  11.8 0.0 copy-done
  11.8 0.3 fusion.15
  12.0 23.9 %all-gather = f32[16,64,16]{1,2,0:T(8,128)S(1)} all-gather(f32[1,64,16]{1,2,0:T(8,128)S(1)} %divide_bitcast_fusion), channel_id=1, replica_groups=mesh['group'=2,'expert'=16,'tensor'=1] {'expert'}, dimensions={0}, use_global_device_ids=true | all-gather | bytes 69632 | tf_op jit(solution)/shard_map/all_gather | solution.py:124
  36.0 0.1 reshape.28
  36.1 46.9 %all-gather.3.cloned.1.call-done = bf16[1024,3584]{1,0:T(8,128)(2,1)} async-done(((bf16[64,3584]{1,0:T(8,128)(2,1)}), bf16[1024,3584]{1,0:T(8,128)(2,1)}) %all-gather.3.cloned.1.call-update) | async-done | bytes 7340048 | tf_op jit(solution)/shard_map/all_gather | solution.py:123
  83.0 12.7 %multiply_convert_fusion.1 = bf16[1024,1024]{1,0:T(8,128)(2,1)S(1)} fusion(bf16[1024,3584]{1,0:T(8,128)(2,1)} %all-gather.3.cloned.1.call-done, bf16[1,3584,1024]{2,1,0:T(8,128)(2,1)} %param.11), kind=kOutput, calls=%fused_computation.5 | convolution fusion | flops 7521435648 | bytes 16777216 | tf_op jit(solution)/shard_map/dot_general | solution.py:127
  95.8 12.9 %multiply_convert_fusion = bf16[1024,3584]{1,0:T(8,128)(2,1)} fusion(bf16[1024,1024]{1,0:T(8,128)(2,1)S(1)} %multiply_convert_fusion.1, bf16[1,3584,1024]{2,1,0:T(8,128)(2,1)} %param.11, f32[1024]{0:T(1024)S(1)} %bitcast.33), kind=kOutput, calls=%fused_computation | convolution fusion | flops 7530872832 | bytes 16781312 | tf_op jit(solution)/shard_map/dot_general | solution.py:130
  108.6 0.0 copy-start.1
  108.6 0.0 copy-start.2
  108.6 0.0 reduce-scatter.2.cloned.1.call-update
  108.7 90.3 %reduce-scatter.2.cloned.1.call-done = bf16[64,3584]{1,0:T(8,128)(2,1)} async-done(((bf16[1024,3584]{1,0:T(8,128)(2,1)}), bf16[64,3584]{1,0:T(8,128)(2,1)}) %reduce-scatter.2.cloned.1.call-update) | async-done | bytes 458768 | tf_op jit(solution)/shard_map/reduce_scatter | solution.py:134
  199.0 0.0 copy-done.1
  199.0 0.0 copy-done.2
  199.0 2.0 add_convert_fusion
  (6 shorter events, 0.1 us)
Async XLA Ops:
  6.5 5.2 %copy-start = (bf16[3584,16]{0,1:T(8,128)(2,1)S(1)}, bf16[3584,16]{0,1:T(8,128)(2,1)}, u32[]{:S(2)}) copy-start(bf16[3584,16]{0,1:T(8,128)(2,1)} %param.9) | copy-start | bytes 344068
  6.5 5.2 %copy-start.3 = (s32[64,8]{0,1:T(8,128)S(1)}, s32[64,8]{0,1:T(8,128)}, u32[]{:S(2)}) copy-start(s32[64,8]{0,1:T(8,128)} %param.10) | copy-start | bytes 6148
  6.5 76.5 %all-gather.3.cloned.1.call-start = ((), (), s32[]{:S(2)}) async-start(), calls=%async_computation.1 | async-start | bytes 7798784 | tf_op jit(solution)/shard_map/all_gather | solution.py:123
  11.7 187.3 %reduce-scatter.2.cloned.1.call-start = ((), (), s32[]{:S(2)}) async-start(), calls=%async_computation.2 | async-start | bytes 7798784 | tf_op jit(solution)/shard_map/reduce_scatter | solution.py:134
  108.6 90.3 %copy-start.1 = (bf16[64,3584]{1,0:T(8,128)(2,1)S(1)}, bf16[64,3584]{1,0:T(8,128)(2,1)}, u32[]{:S(2)}) copy-start(bf16[64,3584]{1,0:T(8,128)(2,1)} %param.6) | copy-start | bytes 1376260
  108.6 90.3 %copy-start.2 = (bf16[1,64,3584]{2,1,0:T(8,128)(2,1)S(1)}, bf16[1,64,3584]{2,1,0:T(8,128)(2,1)}, u32[]{:S(2)}) copy-start(bf16[1,64,3584]{2,1,0:T(8,128)(2,1)} %param.7) | copy-start | bytes 1376260
Sparse Core Ops, SparseCore 0:
  11.8 71.2 all-gather.2
  108.8 90.1 reduce-scatter.1

commit v2 on v1

--- a/solution.py
+++ b/solution.py
@@ -1,6 +1,8 @@
 import jax
 import jax.numpy as jnp
 from jax import lax
+from jax.experimental import pallas as pl
+from jax.experimental.pallas import tpu as pltpu
 from jax.sharding import PartitionSpec as P
 
 QBLOCK = 128
@@ -116,29 +118,270 @@
     return stream, gates, restored
 
 
+def moe_kernel(own_ref, stream_in, weight_hbm, out_ref, rows, weight, stream_ref, share, hidden, core_in, x_in,
+               chain_in, weight_sem, put_sem, line_send, x_send, core_send, row_recv,
+               pair_send, pair_recv, half_send, half_recv, chain_send, chain_recv):
+    block_rows, width = out_ref.shape
+    tile = 256
+    me = lax.axis_index("expert")
+    z, x, c = me // 4, (me // 2) % 2, me % 2
+    flip = z // 2
+    m = z + flip * (3 - 2 * z)
+
+    def expert_at(zz, xx, cc):
+        return (zz * 2 + xx) * 2 + cc
+
+    def place(o):
+        return o + flip * (3 - 2 * o)
+
+    def to(zz, xx, cc):
+        return {"expert": expert_at(zz, xx, cc)}
+
+    def slot(zz, xx, cc):
+        return rows.at[zz, pl.ds(pl.multiple_of(block_rows * (2 * xx + cc), block_rows), block_rows), :]
+
+    barrier = pltpu.get_barrier_semaphore()
+
+    def greet(device):
+        pl.semaphore_signal(barrier, inc=1, device_id=device, device_id_type=pl.DeviceIdType.MESH)
+
+    load_weight = pltpu.make_async_copy(weight_hbm.at[0], weight, weight_sem)
+    load_weight.start()
+    put_own = pltpu.make_async_copy(own_ref, slot(z, x, c), put_sem)
+    put_own.start()
+    greet(to(z, 1 - x, c))
+    greet(to(z, x, 1 - c))
+    pl.when(z > 0)(lambda: greet(to(z - 1, x, c)))
+    pl.when(z < 3)(lambda: greet(to(z + 1, x, c)))
+    put_own.wait()
+    pl.semaphore_wait(barrier, 3 + m)
+
+    def row_copy(zz, xx, cc, sem, device):
+        part = slot(zz, xx, cc)
+        return pltpu.make_async_remote_copy(
+            src_ref=part, dst_ref=part, send_sem=sem, recv_sem=row_recv.at[expert_at(zz, xx, cc)],
+            device_id=device, device_id_type=pl.DeviceIdType.MESH,
+        )
+
+    def up_copy(p):
+        return row_copy(p, x, c, line_send.at[0, p], to(z + 1, x, c))
+
+    def down_copy(p):
+        return row_copy(p, x, c, line_send.at[1, p], to(z - 1, x, c))
+
+    def x_copy(p):
+        return row_copy(p, x, c, x_send.at[p], to(z, 1 - x, c))
+
+    def core_copy(p, xx):
+        return row_copy(p, xx, c, core_send.at[p, xx], to(z, x, 1 - c))
+
+    def got(zz, xx, cc):
+        row_copy(zz, xx, cc, x_send.at[0], to(z, 1 - x, c)).wait_recv()
+
+    def pass_on(p):
+        pl.when((p <= z) & (z < 3))(lambda: up_copy(p).start())
+        pl.when((p >= z) & (z > 0))(lambda: down_copy(p).start())
+        x_copy(p).start()
+        core_copy(p, x).start()
+
+    def arrive_line(p):
+        got(p, x, c)
+        pass_on(p)
+
+    def pair_copy(p):
+        return pltpu.make_async_remote_copy(
+            src_ref=share.at[p, 1 - c], dst_ref=core_in.at[p],
+            send_sem=pair_send.at[p], recv_sem=pair_recv.at[p],
+            device_id=to(z, x, 1 - c), device_id_type=pl.DeviceIdType.MESH,
+        )
+
+    def half_copy(p):
+        return pltpu.make_async_remote_copy(
+            src_ref=share.at[p, c, 1 - x], dst_ref=x_in.at[p],
+            send_sem=half_send.at[p], recv_sem=half_recv.at[p],
+            device_id=to(z, 1 - x, c), device_id_type=pl.DeviceIdType.MESH,
+        )
+
+    def chain_copy(p, towards, index):
+        return pltpu.make_async_remote_copy(
+            src_ref=share.at[p, c, x], dst_ref=chain_in.at[index],
+            send_sem=chain_send.at[p], recv_sem=chain_recv.at[index],
+            device_id=to(towards, x, c), device_id_type=pl.DeviceIdType.MESH,
+        )
+
+    def send_chain(p, act):
+        pl.when(p > z)(lambda: act(chain_copy(p, z + 1, p)))
+        pl.when(p == z - 1)(lambda: act(chain_copy(p, z - 1, 4)))
+        pl.when(p < z - 1)(lambda: act(chain_copy(p, z - 1, p)))
+
+    def compute(p):
+        units = weight.shape[1]
+        gate_block = rows[p, :, width:].astype(jnp.float32)
+        lane = lax.broadcasted_iota(jnp.int32, gate_block.shape, 1)
+        mine = (lane == me) | (lane == me + 64)
+        gate = jnp.sum(jnp.where(mine, gate_block, 0.0), axis=1, keepdims=True)
+
+        def first(n, carry):
+            columns = pl.ds(pl.multiple_of(n * tile, tile), tile)
+            v = jnp.dot(rows[p, :, :width], weight[:, columns], preferred_element_type=jnp.float32)
+            hidden[:, columns] = (v / (1.0 + jnp.exp(-v))).astype(jnp.bfloat16)
+            return carry
+
+        lax.fori_loop(0, units // tile, first, 0)
+
+        def second(n, carry):
+            columns = pl.ds(pl.multiple_of(n * tile, tile), tile)
+            v = lax.dot_general(
+                hidden[...], weight[columns, :], (((1,), (1,)), ((), ())),
+                preferred_element_type=jnp.float32,
+            )
+            v = v.astype(jnp.bfloat16).astype(jnp.float32) * gate
+            v = v.astype(jnp.bfloat16)
+            for i in range(4):
+                share[p, i % 2, i // 2, :, columns] = v[i * block_rows:(i + 1) * block_rows]
+            return carry
+
+        lax.fori_loop(0, width // tile, second, 0)
+
+    def add_pair(p):
+        pair_copy(p).wait_recv()
+        for xx in range(2):
+            share[p, c, xx] = (
+                share[p, c, xx].astype(jnp.float32) + core_in[p, xx].astype(jnp.float32)
+            ).astype(jnp.bfloat16)
+        half_copy(p).start()
+
+    def add_half(p):
+        half_copy(p).wait_recv()
+        has = ((p > z) & (z > 0)) | ((p < z) & (z < 3))
+
+        @pl.when(has)
+        def _():
+            chain_copy(p, z, p).wait_recv()
+            share[p, c, x] = (
+                share[p, c, x].astype(jnp.float32) + x_in[p].astype(jnp.float32)
+                + chain_in[p].astype(jnp.float32)
+            ).astype(jnp.bfloat16)
+
+        @pl.when(jnp.logical_not(has))
+        def _():
+            share[p, c, x] = (
+                share[p, c, x].astype(jnp.float32) + x_in[p].astype(jnp.float32)
+            ).astype(jnp.bfloat16)
+
+        send_chain(p, lambda copy: copy.start())
+
+    pass_on(z)
+    middle = m == 1
+
+    def step(k, carry):
+        own_order = jnp.where(k == 0, m, jnp.where(k == 1, 1 - m, k))
+        p = place(own_order)
+        later = place(jnp.where(k == 0, 1 - m, k + 1))
+        pl.when(k < 3 - 2 * m)(lambda: arrive_line(later))
+        pl.when(middle & (k == 0))(lambda: arrive_line(place(2)))
+        pl.when(middle & (k == 1))(lambda: arrive_line(place(3)))
+        got(p, 1 - x, c)
+        core_copy(p, 1 - x).start()
+        pl.when(k == 3)(lambda: add_pair(place(2)))
+        got(p, x, 1 - c)
+        got(p, 1 - x, 1 - c)
+        pl.when(k == 0)(lambda: load_weight.wait())
+        compute(p)
+        pair_copy(p).start()
+        return carry
+
+    lax.fori_loop(0, 4, step, 0)
+
+    order = [place(2), place(3), place(1 - m), z]
+    add_pair(order[1])
+    add_half(order[0])
+    add_pair(order[2])
+    add_half(order[1])
+    add_pair(order[3])
+    add_half(order[2])
+    half_copy(z).wait_recv()
+    share_sum = share[z, c, x].astype(jnp.float32) + x_in[z].astype(jnp.float32)
+    out_sum = stream_in[...] + share_sum
+    stream_ref[...] = out_sum
+
+    @pl.when(z > 0)
+    def _():
+        chain_copy(z, z, z).wait_recv()
+        stream_ref[...] += chain_in[z].astype(jnp.float32)
+
+    @pl.when(z < 3)
+    def _():
+        chain_copy(z, z, 4).wait_recv()
+        stream_ref[...] += chain_in[4].astype(jnp.float32)
+
+    out_ref[...] = stream_ref[...].astype(out_ref.dtype)
+
+    def settle(p, carry):
+        pl.when((p <= z) & (z < 3))(lambda: up_copy(p).wait_send())
+        pl.when((p >= z) & (z > 0))(lambda: down_copy(p).wait_send())
+        x_copy(p).wait_send()
+        core_copy(p, 0).wait_send()
+        core_copy(p, 1).wait_send()
+        pair_copy(p).wait_send()
+        half_copy(p).wait_send()
+        send_chain(p, lambda copy: copy.wait_send())
+        return carry
+
+    lax.fori_loop(0, 4, settle, 0)
+
+
+def exchange(own, stream, expert_weight):
+    block_rows, width = stream.shape
+    wide = own.shape[1]
+    units = expert_weight.shape[2]
+    vmem = pl.BlockSpec(memory_space=pltpu.VMEM)
+    rows_all = 16 * block_rows
+    dma = pltpu.SemaphoreType.DMA
+    return pl.pallas_call(
+        moe_kernel,
+        out_shape=jax.ShapeDtypeStruct((block_rows, width), jnp.bfloat16),
+        in_specs=[vmem, vmem, pl.BlockSpec(memory_space=pl.ANY)],
+        out_specs=vmem,
+        scratch_shapes=[
+            pltpu.VMEM((4, 4 * block_rows, wide), jnp.bfloat16),
+            pltpu.VMEM((width, units), jnp.bfloat16),
+            pltpu.VMEM((block_rows, width), jnp.float32),
+            pltpu.VMEM((4, 2, 2, block_rows, width), jnp.bfloat16),
+            pltpu.VMEM((4 * block_rows, units), jnp.bfloat16),
+            pltpu.VMEM((4, 2, block_rows, width), jnp.bfloat16),
+            pltpu.VMEM((4, block_rows, width), jnp.bfloat16),
+            pltpu.VMEM((5, block_rows, width), jnp.bfloat16),
+            dma, dma, dma((2, 4)), dma((4,)), dma((4, 2)), dma((16,)),
+            dma((4,)), dma((4,)), dma((4,)), dma((4,)), dma((4,)), dma((5,)),
+        ],
+        compiler_params=pltpu.CompilerParams(
+            collective_id=0, has_side_effects=True, vmem_limit_bytes=56 * 1024 * 1024
+        ),
+        cost_estimate=pl.CostEstimate(
+            flops=4 * rows_all * width * units,
+            bytes_accessed=2 * width * units + 16 * block_rows * width,
+            transcendentals=rows_all * units,
+        ),
+    )(own, stream, expert_weight)
+
+
 def local_dense(residual, attn_partial, norm_gain, router_weight, expert_ids, expert_weight):
     stream, gates, restored = local_rows(
         residual, attn_partial, norm_gain, router_weight, expert_ids
     )
-    rows = lax.all_gather(restored, "expert", axis=0, tiled=True)
-    all_gates = lax.all_gather(gates, "expert", axis=0, tiled=True)
-    gate = lax.dynamic_slice_in_dim(all_gates, lax.axis_index("expert"), 1, 1)
-    w_expert = expert_weight[0]
-    hidden = jax.nn.silu(jnp.dot(rows, w_expert, preferred_element_type=jnp.float32)).astype(
-        jnp.bfloat16
-    )
-    output = lax.dot_general(
-        hidden, w_expert, (((1,), (1,)), ((), ())), preferred_element_type=jnp.float32
-    ).astype(jnp.bfloat16)
-    share = (output.astype(jnp.float32) * gate).astype(jnp.bfloat16)
-    moe = lax.psum_scatter(share, "expert", scatter_dimension=0, tiled=True)
-    return (stream + moe.astype(jnp.float32)).astype(jnp.bfloat16)
+    expert_count = gates.shape[1]
+    high = gates.astype(jnp.bfloat16)
+    low = (gates - high.astype(jnp.float32)).astype(jnp.bfloat16)
+    spare = jnp.zeros((gates.shape[0], 64 - expert_count), jnp.bfloat16)
+    own = jnp.concatenate([restored, high, spare, low, spare], axis=1)
+    return exchange(own, stream, expert_weight)
 
 
 def dense_fits(mesh, row_count, expert_count, top_count):
     return (
         mesh.shape["tensor"] == 1
-        and mesh.shape["expert"] == expert_count
+        and mesh.shape["expert"] == expert_count == 16
         and expert_count <= 4 * top_count
     )
 

time: 208 us -> 118 us (0.57)
  waiting for transfers between devices: 137 us -> 0 us
  Pallas kernels: 0 us -> 109 us
  matrix products: 25.8 us -> 0.36 us
  blocking collectives: 23.9 us -> 0 us
  between operations: 13.5 us -> 0.09 us
  local copies, waits for them, and re-layouts: 0.69 us -> 3.32 us
    pallas_call x0 -> x1, Pallas kernels: none -> 109 us  [exchange(): pl.pallas_call(moe_kernel, out_shape=jax.ShapeDtypeStruct((block_rows, wi...]
    reduce_scatter x1 -> x0, waiting for transfers between devices: 90.3 us -> none  [local_dense(): moe = lax.psum_scatter(share, 'expert', scatter_dimension=0, tiled=True)]
    all_gather x1 -> x0, waiting for transfers between devices: 46.9 us -> none  [local_dense(): rows = lax.all_gather(restored, 'expert', axis=0, tiled=True)]
    dot_general x2 -> x0, matrix products: 25.6 us -> none  [the longest x1 12.9 us: local_dense(): lax.dot_general(hidden, w_expert, (((1,), (1,)), ((), ())), preferred_ele...]
    all_gather x1 -> x0, blocking collectives: 23.9 us -> none  [local_dense(): all_gates = lax.all_gather(gates, 'expert', axis=0, tiled=True)]
    add x0 -> x1, other arithmetic: none -> 2.38 us  [local_rows(): stream = residual.astype(jnp.float32) + attn_partial[0].astype(jnp.float32)]
  transfers between devices with their start and end apart: 2 -> 0, of which waited for: 2 -> 0; matrix products, arithmetic and copies ran while one was open for 0% -> 0% of each run, Pallas kernels for 0% -> 0%
where the time goes in v2:
time: 118 us
  Pallas kernels  109 us (92%)
  other arithmetic  4.89 us (4%)
  local copies, waits for them, and re-layouts  3.32 us (3%)
    pallas_call x1, Pallas kernels, exchange(): pl.pallas_call(moe_kernel, out_shape=jax.ShapeDtypeStruct((block_rows, wi...  109 us
    add x1, other arithmetic, local_rows(): stream = residual.astype(jnp.float32) + attn_partial[0].astype(jnp.float32)  2.38 us

profile of v2, /device:TPU:0, one launch (start us, length us, event | category | flops | bytes accessed | tf_op | source)
XLA Modules:
  0.0 117.9 jit_solution(1451742328066863554)
XLA Ops:
  0.0 0.0 copy-start
  0.0 0.0 copy-start.1
  0.0 2.4 %convert_add_fusion = (f32[64,3584]{1,0:T(8,128)}, f32[64]{0:T(128)S(1)}) fusion(bf16[64,3584]{1,0:T(8,128)(2,1)} %param.6, bf16[1,64,3584]{2,1,0:T(8,128)(2,1)} %param.7), kind=kLoop, calls=%fused_computation.10 | loop fusion | flops 1146816 | bytes 1835264 | tf_op jit(solution)/shard_map/add | solution.py:108
  2.4 1.4 %convert_abs_fusion = (f32[64,3584]{1,0:T(8,128)S(1)}, bf16[64,3584]{1,0:T(8,128)(2,1)S(1)}) fusion(f32[3584]{0:T(1024)} %param.8, f32[64]{0:T(128)S(1)} %add_rsqrt_fusion, bf16[1,64,3584]{2,1,0:T(8,128)(2,1)} %param.7, bf16[64,3584]{1,0:T(8,128)(2,1)} %param.6), kind=kLoop, calls=%fused_computation.1 | loop fusion | flops 1835008 | bytes 2308352 | tf_op jit(solution)/shard_map/abs | solution.py:18
  3.8 0.2 abs.7
  4.0 0.3 reduce_max.9
  4.4 0.3 div.38
  4.7 0.7 fusion.5
  5.4 0.0 copy-done.1
  5.4 0.1 copy.14
  5.5 0.0 copy-done
  5.5 0.4 fusion.9
  5.8 0.1 subtract_convert_fusion
  6.0 0.9 concatenate.3.own_ref
  6.8 109.3 %shard_map.64 = bf16[64,3584]{1,0:T(8,128)(2,1)} custom-call(bf16[64,3712]{1,0:T(8,128)(2,1)} %concatenate.3.own_ref, f32[64,3584]{1,0:T(8,128)} %get-tuple-element.7.stream_in, bf16[1,3584,1024]{2,1,0:T(8,128)(2,1)} %weight_hbm.1), custom_call_target="tpu_custom_call" | custom-call | flops 15032385536 | bytes 11010048 | tf_op jit(solution)/shard_map/pallas_call | solution.py:341
  116.1 1.8 %copy.24 = bf16[64,3584]{1,0:T(8,128)(2,1)} copy(bf16[64,3584]{1,0:T(8,128)(2,1)} %shard_map.64) | data formatting | bytes 917504
  (4 shorter events, 0.0 us)
Async XLA Ops:
  0.0 5.5 %copy-start = (bf16[3584,16]{0,1:T(8,128)(2,1)S(1)}, bf16[3584,16]{0,1:T(8,128)(2,1)}, u32[]{:S(2)}) copy-start(bf16[3584,16]{0,1:T(8,128)(2,1)} %param.9) | copy-start | bytes 344068
  0.0 5.4 %copy-start.1 = (s32[64,8]{0,1:T(8,128)S(1)}, s32[64,8]{0,1:T(8,128)}, u32[]{:S(2)}) copy-start(s32[64,8]{0,1:T(8,128)} %param.10) | copy-start | bytes 6148

commit v3 on v2

--- a/solution.py
+++ b/solution.py
@@ -103,23 +103,8 @@
     return (stream_share + moe_share).astype(jnp.bfloat16)
 
 
-def local_rows(residual, attn_partial, norm_gain, router_weight, expert_ids):
-    expert_count = router_weight.shape[1]
-    stream = residual.astype(jnp.float32) + attn_partial[0].astype(jnp.float32)
-    meansq = jnp.mean(stream * stream, axis=1, keepdims=True)
-    normed = (stream * lax.rsqrt(meansq + EPS) * norm_gain).astype(jnp.bfloat16)
-    logits = jnp.dot(normed, router_weight, preferred_element_type=jnp.float32)
-    affinity = jax.nn.sigmoid(logits)
-    chosen = expert_ids[:, :, None] == jnp.arange(expert_count, dtype=jnp.int32)[None, None, :]
-    picked = jnp.where(jnp.any(chosen, axis=1), affinity, 0.0)
-    gates = ROUTE_SCALE * picked / jnp.sum(picked, axis=1, keepdims=True)
-    encoded, block_scale = encode(normed)
-    restored = decode(encoded, block_scale)
-    return stream, gates, restored
-
-
-def moe_kernel(own_ref, stream_in, weight_hbm, out_ref, rows, weight, stream_ref, share, hidden, core_in, x_in,
-               chain_in, weight_sem, put_sem, line_send, x_send, core_send, row_recv,
+def moe_kernel(residual_ref, attn_ref, gain_ref, router_ref, ids_ref, weight_hbm, out_ref, rows, weight, stream_ref, stage, share, hidden, core_in, x_in,
+               chain_in, weight_sem, line_send, x_send, core_send, row_recv,
                pair_send, pair_recv, half_send, half_recv, chain_send, chain_recv):
     block_rows, width = out_ref.shape
     tile = 256
@@ -147,13 +132,39 @@
 
     load_weight = pltpu.make_async_copy(weight_hbm.at[0], weight, weight_sem)
     load_weight.start()
-    put_own = pltpu.make_async_copy(own_ref, slot(z, x, c), put_sem)
-    put_own.start()
     greet(to(z, 1 - x, c))
     greet(to(z, x, 1 - c))
     pl.when(z > 0)(lambda: greet(to(z - 1, x, c)))
     pl.when(z < 3)(lambda: greet(to(z + 1, x, c)))
-    put_own.wait()
+    stream = residual_ref[...].astype(jnp.float32) + attn_ref[0].astype(jnp.float32)
+    stream_ref[...] = stream
+    meansq = jnp.sum(stream * stream, axis=1, keepdims=True) * (1.0 / width)
+    inverse = lax.rsqrt(meansq + EPS)
+    own = pl.ds(pl.multiple_of(block_rows * (2 * x + c), block_rows), block_rows)
+    expert_count = router_ref.shape[1]
+    for b in range(width // QBLOCK):
+        cols = slice(b * QBLOCK, (b + 1) * QBLOCK)
+        normed = (stream_ref[:, cols] * inverse * gain_ref[:, cols]).astype(jnp.bfloat16)
+        rows[z, own, cols] = normed
+        values = normed.astype(jnp.float32)
+        largest = jnp.max(jnp.abs(values), axis=1, keepdims=True)
+        scale = ((largest + EPS) / 448.0).astype(jnp.bfloat16).astype(jnp.float32)
+        encoded = (values / scale).astype(jnp.bfloat16)
+        stage[:, cols] = (encoded.astype(jnp.float32) * scale).astype(jnp.bfloat16)
+    logits = jnp.dot(
+        rows[z, own, :width], router_ref[...], preferred_element_type=jnp.float32
+    )
+    rows[z, own, :width] = stage[...]
+    affinity = 1.0 / (1.0 + jnp.exp(-logits))
+    expert = lax.broadcasted_iota(jnp.int32, logits.shape, 1)
+    picked = jnp.zeros_like(affinity)
+    for j in range(ids_ref.shape[1]):
+        picked += jnp.where(ids_ref[:, j:j + 1] == expert, affinity, 0.0)
+    gates = ROUTE_SCALE * picked / jnp.sum(picked, axis=1, keepdims=True)
+    high = gates.astype(jnp.bfloat16).astype(jnp.float32)
+    spare = jnp.zeros((block_rows, 64 - expert_count), jnp.float32)
+    wide_gates = jnp.concatenate([high, spare, gates - high, spare], axis=1)
+    rows[z, own, width:] = wide_gates.astype(jnp.bfloat16)
     pl.semaphore_wait(barrier, 3 + m)
 
     def row_copy(zz, xx, cc, sem, device):
@@ -302,7 +313,7 @@
     add_half(order[2])
     half_copy(z).wait_recv()
     share_sum = share[z, c, x].astype(jnp.float32) + x_in[z].astype(jnp.float32)
-    out_sum = stream_in[...] + share_sum
+    out_sum = stream_ref[...] + share_sum
     stream_ref[...] = out_sum
 
     @pl.when(z > 0)
@@ -331,9 +342,9 @@
     lax.fori_loop(0, 4, settle, 0)
 
 
-def exchange(own, stream, expert_weight):
-    block_rows, width = stream.shape
-    wide = own.shape[1]
+def exchange(residual, attn_partial, norm_gain, router_weight, expert_ids, expert_weight):
+    block_rows, width = residual.shape
+    wide = width + 128
     units = expert_weight.shape[2]
     vmem = pl.BlockSpec(memory_space=pltpu.VMEM)
     rows_all = 16 * block_rows
@@ -341,18 +352,19 @@
     return pl.pallas_call(
         moe_kernel,
         out_shape=jax.ShapeDtypeStruct((block_rows, width), jnp.bfloat16),
-        in_specs=[vmem, vmem, pl.BlockSpec(memory_space=pl.ANY)],
+        in_specs=[vmem] * 5 + [pl.BlockSpec(memory_space=pl.ANY)],
         out_specs=vmem,
         scratch_shapes=[
             pltpu.VMEM((4, 4 * block_rows, wide), jnp.bfloat16),
             pltpu.VMEM((width, units), jnp.bfloat16),
             pltpu.VMEM((block_rows, width), jnp.float32),
+            pltpu.VMEM((block_rows, width), jnp.bfloat16),
             pltpu.VMEM((4, 2, 2, block_rows, width), jnp.bfloat16),
             pltpu.VMEM((4 * block_rows, units), jnp.bfloat16),
             pltpu.VMEM((4, 2, block_rows, width), jnp.bfloat16),
             pltpu.VMEM((4, block_rows, width), jnp.bfloat16),
             pltpu.VMEM((5, block_rows, width), jnp.bfloat16),
-            dma, dma, dma((2, 4)), dma((4,)), dma((4, 2)), dma((16,)),
+            dma, dma((2, 4)), dma((4,)), dma((4, 2)), dma((16,)),
             dma((4,)), dma((4,)), dma((4,)), dma((4,)), dma((4,)), dma((5,)),
         ],
         compiler_params=pltpu.CompilerParams(
@@ -363,19 +375,7 @@
             bytes_accessed=2 * width * units + 16 * block_rows * width,
             transcendentals=rows_all * units,
         ),
-    )(own, stream, expert_weight)
-
-
-def local_dense(residual, attn_partial, norm_gain, router_weight, expert_ids, expert_weight):
-    stream, gates, restored = local_rows(
-        residual, attn_partial, norm_gain, router_weight, expert_ids
-    )
-    expert_count = gates.shape[1]
-    high = gates.astype(jnp.bfloat16)
-    low = (gates - high.astype(jnp.float32)).astype(jnp.bfloat16)
-    spare = jnp.zeros((gates.shape[0], 64 - expert_count), jnp.bfloat16)
-    own = jnp.concatenate([restored, high, spare, low, spare], axis=1)
-    return exchange(own, stream, expert_weight)
+    )(residual, attn_partial, norm_gain[None, :], router_weight, expert_ids, expert_weight)
 
 
 def dense_fits(mesh, row_count, expert_count, top_count):
@@ -399,7 +399,7 @@
     def run(residual, attn_partial, norm_gain, router_weight, expert_ids, expert_weight):
         dense = dense_fits(mesh, residual.shape[0], router_weight.shape[1], expert_ids.shape[1])
         return jax.shard_map(
-            local_dense if dense else local,
+            exchange if dense else local,
             mesh=mesh,
             in_specs=placed,
             out_specs=P(("group", "expert"), "tensor"),

time: 118 us -> 117 us (level)
  other arithmetic: 4.89 us -> 0 us
  local copies, waits for them, and re-layouts: 3.32 us -> 6.66 us
    unnamed x5 -> x3, local copies, waits for them, and re-layouts: 1.82 us -> 5.34 us
    add x1 -> x0, other arithmetic: 2.38 us -> none  [local_rows(): stream = residual.astype(jnp.float32) + attn_partial[0].astype(jnp.float32)]
    abs x1 -> x0, other arithmetic: 1.4 us -> none  [encode(): largest = jnp.max(jnp.abs(blocks), axis=-1)]
    broadcast_in_dim x1, local copies, waits for them, and re-layouts: 0.01 us -> 1.33 us  [exchange(): norm_gain[None, :]]
where the time goes in v3:
time: 117 us
  Pallas kernels  110 us (94%)
  local copies, waits for them, and re-layouts  6.66 us (6%)
    pallas_call x1, Pallas kernels, exchange(): pl.pallas_call(moe_kernel, out_shape=jax.ShapeDtypeStruct((block_rows, wi...  110 us
    unnamed x3, local copies, waits for them, and re-layouts  5.34 us

profile of v3, /device:TPU:0, one launch (start us, length us, event | category | flops | bytes accessed | tf_op | source)
XLA Modules:
  0.0 116.7 jit_solution(5120516512029474715)
XLA Ops:
  0.0 1.3 %broadcast_in_dim.3.gain_ref = f32[1,3584]{1,0:T(1,128)} reshape(f32[3584]{0:T(1024)} %param.8) | data formatting | bytes 28672 | tf_op jit(solution)/shard_map/broadcast_in_dim | solution.py:378
  1.3 1.4 %copy.8.ids_ref = s32[64,8]{1,0:T(8,128)} copy(s32[64,8]{0,1:T(8,128)} %param.10) | data formatting | bytes 4096 | tf_op args[4]
  2.7 2.1 %copy.7.router_ref = bf16[3584,16]{1,0:T(8,128)(2,1)} copy(bf16[3584,16]{0,1:T(8,128)(2,1)} %param.9) | data formatting | bytes 229376 | tf_op args[3]
  4.8 110.0 %shard_map.64 = bf16[64,3584]{1,0:T(8,128)(2,1)} custom-call(bf16[64,3584]{1,0:T(8,128)(2,1)} %residual_ref.1, bf16[1,64,3584]{2,1,0:T(8,128)(2,1)} %attn_ref.1, f32[1,3584]{1,0:T(1,128)} %broadcast_in_dim.3.gain_ref, bf16[3584,16]{1,0:T(8,128)(2,1)} %copy.7.router_ref, s32[64,8]{1,0:T(8,128)} %copy.8.ids_ref, bf16[1,3584,1024]{2,1,0:T(8,128)(2,1)} %weight_hbm.1), custom_call_target="tpu_custom_call" | custom-call | flops 15032385536 | bytes 11010048 | tf_op jit(solution)/shard_map/pallas_call | solution.py:352
  114.9 1.8 %copy.10 = bf16[64,3584]{1,0:T(8,128)(2,1)} copy(bf16[64,3584]{1,0:T(8,128)(2,1)} %shard_map.64) | data formatting | bytes 917504

commit v4 on v3

--- a/solution.py
+++ b/solution.py
@@ -199,6 +199,11 @@
         got(p, x, c)
         pass_on(p)
 
+    half = width // 256 * 128
+
+    def piece(h):
+        return pl.ds(0, half) if h == 0 else pl.ds(half, width - half)
+
     def pair_copy(p):
         return pltpu.make_async_remote_copy(
             src_ref=share.at[p, 1 - c], dst_ref=core_in.at[p],
@@ -206,24 +211,24 @@
             device_id=to(z, x, 1 - c), device_id_type=pl.DeviceIdType.MESH,
         )
 
-    def half_copy(p):
+    def half_copy(p, h):
         return pltpu.make_async_remote_copy(
-            src_ref=share.at[p, c, 1 - x], dst_ref=x_in.at[p],
-            send_sem=half_send.at[p], recv_sem=half_recv.at[p],
+            src_ref=share.at[p, c, 1 - x, :, piece(h)], dst_ref=x_in.at[p, :, piece(h)],
+            send_sem=half_send.at[h, p], recv_sem=half_recv.at[h, p],
             device_id=to(z, 1 - x, c), device_id_type=pl.DeviceIdType.MESH,
         )
 
-    def chain_copy(p, towards, index):
+    def chain_copy(p, towards, index, h):
         return pltpu.make_async_remote_copy(
-            src_ref=share.at[p, c, x], dst_ref=chain_in.at[index],
-            send_sem=chain_send.at[p], recv_sem=chain_recv.at[index],
+            src_ref=share.at[p, c, x, :, piece(h)], dst_ref=chain_in.at[index, :, piece(h)],
+            send_sem=chain_send.at[h, p], recv_sem=chain_recv.at[h, index],
             device_id=to(towards, x, c), device_id_type=pl.DeviceIdType.MESH,
         )
 
-    def send_chain(p, act):
-        pl.when(p > z)(lambda: act(chain_copy(p, z + 1, p)))
-        pl.when(p == z - 1)(lambda: act(chain_copy(p, z - 1, 4)))
-        pl.when(p < z - 1)(lambda: act(chain_copy(p, z - 1, p)))
+    def send_chain(p, h, act):
+        pl.when(p > z)(lambda: act(chain_copy(p, z + 1, p, h)))
+        pl.when(p == z - 1)(lambda: act(chain_copy(p, z - 1, 4, h)))
+        pl.when(p < z - 1)(lambda: act(chain_copy(p, z - 1, p, h)))
 
     def compute(p):
         units = weight.shape[1]
@@ -256,31 +261,36 @@
 
     def add_pair(p):
         pair_copy(p).wait_recv()
-        for xx in range(2):
-            share[p, c, xx] = (
-                share[p, c, xx].astype(jnp.float32) + core_in[p, xx].astype(jnp.float32)
-            ).astype(jnp.bfloat16)
-        half_copy(p).start()
-
-    def add_half(p):
-        half_copy(p).wait_recv()
+        share[p, c, 1 - x] = (
+            share[p, c, 1 - x].astype(jnp.float32) + core_in[p, 1 - x].astype(jnp.float32)
+        ).astype(jnp.bfloat16)
+        half_copy(p, 0).start()
+        half_copy(p, 1).start()
+
+    def add_half(p, h):
+        cols = piece(h)
+        half_copy(p, h).wait_recv()
         has = ((p > z) & (z > 0)) | ((p < z) & (z < 3))
+
+        def total():
+            return (
+                share[p, c, x, :, cols].astype(jnp.float32)
+                + core_in[p, x, :, cols].astype(jnp.float32)
+                + x_in[p, :, cols].astype(jnp.float32)
+            )
 
         @pl.when(has)
         def _():
-            chain_copy(p, z, p).wait_recv()
-            share[p, c, x] = (
-                share[p, c, x].astype(jnp.float32) + x_in[p].astype(jnp.float32)
-                + chain_in[p].astype(jnp.float32)
+            chain_copy(p, z, p, h).wait_recv()
+            share[p, c, x, :, cols] = (
+                total() + chain_in[p, :, cols].astype(jnp.float32)
             ).astype(jnp.bfloat16)
 
         @pl.when(jnp.logical_not(has))
         def _():
-            share[p, c, x] = (
-                share[p, c, x].astype(jnp.float32) + x_in[p].astype(jnp.float32)
-            ).astype(jnp.bfloat16)
-
-        send_chain(p, lambda copy: copy.start())
+            share[p, c, x, :, cols] = total().astype(jnp.bfloat16)
+
+        send_chain(p, h, lambda copy: copy.start())
 
     pass_on(z)
     middle = m == 1
@@ -306,27 +316,33 @@
 
     order = [place(2), place(3), place(1 - m), z]
     add_pair(order[1])
-    add_half(order[0])
+    add_half(order[0], 0)
+    add_half(order[0], 1)
     add_pair(order[2])
-    add_half(order[1])
+    add_half(order[1], 0)
+    add_half(order[1], 1)
     add_pair(order[3])
-    add_half(order[2])
-    half_copy(z).wait_recv()
-    share_sum = share[z, c, x].astype(jnp.float32) + x_in[z].astype(jnp.float32)
-    out_sum = stream_ref[...] + share_sum
-    stream_ref[...] = out_sum
-
-    @pl.when(z > 0)
-    def _():
-        chain_copy(z, z, z).wait_recv()
-        stream_ref[...] += chain_in[z].astype(jnp.float32)
-
-    @pl.when(z < 3)
-    def _():
-        chain_copy(z, z, 4).wait_recv()
-        stream_ref[...] += chain_in[4].astype(jnp.float32)
-
-    out_ref[...] = stream_ref[...].astype(out_ref.dtype)
+    add_half(order[2], 0)
+    add_half(order[2], 1)
+    for h in range(2):
+        cols = piece(h)
+        half_copy(z, h).wait_recv()
+        stream_ref[:, cols] += (
+            share[z, c, x, :, cols].astype(jnp.float32)
+            + core_in[z, x, :, cols].astype(jnp.float32)
+            + x_in[z, :, cols].astype(jnp.float32)
+        )
+
+    for h in range(2):
+        cols = piece(h)
+
+        def add_chain(index, cols=cols, h=h):
+            chain_copy(z, z, index, h).wait_recv()
+            stream_ref[:, cols] += chain_in[index, :, cols].astype(jnp.float32)
+
+        pl.when(z > 0)(lambda f=add_chain: f(z))
+        pl.when(z < 3)(lambda f=add_chain: f(4))
+        out_ref[:, cols] = stream_ref[:, cols].astype(out_ref.dtype)
 
     def settle(p, carry):
         pl.when((p <= z) & (z < 3))(lambda: up_copy(p).wait_send())
@@ -335,8 +351,9 @@
         core_copy(p, 0).wait_send()
         core_copy(p, 1).wait_send()
         pair_copy(p).wait_send()
-        half_copy(p).wait_send()
-        send_chain(p, lambda copy: copy.wait_send())
+        for h in range(2):
+            half_copy(p, h).wait_send()
+            send_chain(p, h, lambda copy: copy.wait_send())
         return carry
 
     lax.fori_loop(0, 4, settle, 0)
@@ -365,7 +382,7 @@
             pltpu.VMEM((4, block_rows, width), jnp.bfloat16),
             pltpu.VMEM((5, block_rows, width), jnp.bfloat16),
             dma, dma((2, 4)), dma((4,)), dma((4, 2)), dma((16,)),
-            dma((4,)), dma((4,)), dma((4,)), dma((4,)), dma((4,)), dma((5,)),
+            dma((4,)), dma((4,)), dma((2, 4)), dma((2, 4)), dma((2, 4)), dma((2, 5)),
         ],
         compiler_params=pltpu.CompilerParams(
             collective_id=0, has_side_effects=True, vmem_limit_bytes=56 * 1024 * 1024

time: 117 us -> 105 us (0.90)
  Pallas kernels: 110 us -> 98.4 us
    pallas_call x1, Pallas kernels: 110 us -> 98.4 us  [exchange(): pl.pallas_call(moe_kernel, out_shape=jax.ShapeDtypeStruct((block_rows, wi...]
where the time goes in v4:
time: 105 us
  Pallas kernels  98.4 us (94%)
  local copies, waits for them, and re-layouts  6.66 us (6%)
    pallas_call x1, Pallas kernels, exchange(): pl.pallas_call(moe_kernel, out_shape=jax.ShapeDtypeStruct((block_rows, wi...  98.4 us
    unnamed x3, local copies, waits for them, and re-layouts  5.34 us

profile of v4, /device:TPU:0, one launch (start us, length us, event | category | flops | bytes accessed | tf_op | source)
XLA Modules:
  0.0 105.1 jit_solution(13654583628584297466)
XLA Ops:
  0.0 1.3 %broadcast_in_dim.3.gain_ref = f32[1,3584]{1,0:T(1,128)} reshape(f32[3584]{0:T(1024)} %param.8) | data formatting | bytes 28672 | tf_op jit(solution)/shard_map/broadcast_in_dim | solution.py:395
  1.3 1.4 %copy.8.ids_ref = s32[64,8]{1,0:T(8,128)} copy(s32[64,8]{0,1:T(8,128)} %param.10) | data formatting | bytes 4096 | tf_op args[4]
  2.7 2.1 %copy.7.router_ref = bf16[3584,16]{1,0:T(8,128)(2,1)} copy(bf16[3584,16]{0,1:T(8,128)(2,1)} %param.9) | data formatting | bytes 229376 | tf_op args[3]
  4.8 98.4 %shard_map.64 = bf16[64,3584]{1,0:T(8,128)(2,1)} custom-call(bf16[64,3584]{1,0:T(8,128)(2,1)} %residual_ref.1, bf16[1,64,3584]{2,1,0:T(8,128)(2,1)} %attn_ref.1, f32[1,3584]{1,0:T(1,128)} %broadcast_in_dim.3.gain_ref, bf16[3584,16]{1,0:T(8,128)(2,1)} %copy.7.router_ref, s32[64,8]{1,0:T(8,128)} %copy.8.ids_ref, bf16[1,3584,1024]{2,1,0:T(8,128)(2,1)} %weight_hbm.1), custom_call_target="tpu_custom_call" | custom-call | flops 15032385536 | bytes 11010048 | tf_op jit(solution)/shard_map/pallas_call | solution.py:369
  103.3 1.8 %copy.10 = bf16[64,3584]{1,0:T(8,128)(2,1)} copy(bf16[64,3584]{1,0:T(8,128)(2,1)} %shard_map.64) | data formatting | bytes 917504

commit v5 on v4

--- a/solution.py
+++ b/solution.py
@@ -316,9 +316,9 @@
 
     order = [place(2), place(3), place(1 - m), z]
     add_pair(order[1])
+    add_pair(order[2])
     add_half(order[0], 0)
     add_half(order[0], 1)
-    add_pair(order[2])
     add_half(order[1], 0)
     add_half(order[1], 1)
     add_pair(order[3])

time: 105 us -> 105 us (level)
  no operation moved by 1% of the time
where the time goes in v5:
time: 105 us
  Pallas kernels  98.5 us (94%)
  local copies, waits for them, and re-layouts  6.66 us (6%)
    pallas_call x1, Pallas kernels, exchange(): pl.pallas_call(moe_kernel, out_shape=jax.ShapeDtypeStruct((block_rows, wi...  98.5 us
    unnamed x3, local copies, waits for them, and re-layouts  5.34 us

profile of v5, /device:TPU:0, one launch (start us, length us, event | category | flops | bytes accessed | tf_op | source)
XLA Modules:
  0.0 105.2 jit_solution(11564535270866139197)
XLA Ops:
  0.0 1.3 %broadcast_in_dim.3.gain_ref = f32[1,3584]{1,0:T(1,128)} reshape(f32[3584]{0:T(1024)} %param.8) | data formatting | bytes 28672 | tf_op jit(solution)/shard_map/broadcast_in_dim | solution.py:395
  1.3 1.4 %copy.8.ids_ref = s32[64,8]{1,0:T(8,128)} copy(s32[64,8]{0,1:T(8,128)} %param.10) | data formatting | bytes 4096 | tf_op args[4]
  2.7 2.1 %copy.7.router_ref = bf16[3584,16]{1,0:T(8,128)(2,1)} copy(bf16[3584,16]{0,1:T(8,128)(2,1)} %param.9) | data formatting | bytes 229376 | tf_op args[3]
  4.8 98.5 %shard_map.64 = bf16[64,3584]{1,0:T(8,128)(2,1)} custom-call(bf16[64,3584]{1,0:T(8,128)(2,1)} %residual_ref.1, bf16[1,64,3584]{2,1,0:T(8,128)(2,1)} %attn_ref.1, f32[1,3584]{1,0:T(1,128)} %broadcast_in_dim.3.gain_ref, bf16[3584,16]{1,0:T(8,128)(2,1)} %copy.7.router_ref, s32[64,8]{1,0:T(8,128)} %copy.8.ids_ref, bf16[1,3584,1024]{2,1,0:T(8,128)(2,1)} %weight_hbm.1), custom_call_target="tpu_custom_call" | custom-call | flops 15032385536 | bytes 11010048 | tf_op jit(solution)/shard_map/pallas_call | solution.py:369
  103.4 1.8 %copy.10 = bf16[64,3584]{1,0:T(8,128)(2,1)} copy(bf16[64,3584]{1,0:T(8,128)(2,1)} %shard_map.64) | data formatting | bytes 917504
